TPU v7x, 32 devices: a whole 2x2x4 slice. The times are simulated.
32 devices in a mesh: groups: 2 (over y), blk: 16 (over z, x, core).
Axes of the slice: x: 2, y: 2, z: 4, core: 2. Of those that a mesh axis runs over, the one named last changes fastest.
Arguments:
- snapshots: bfloat16 [64, 64, 16, 128], P(None, ('groups', 'blk')), parts along dimension 1, may hold values from -200 to 200
- old_modes: bfloat16 [192, 64, 16, 128], P(None, ('groups', 'blk')), parts along dimension 1, may hold values from -60 to 60
- mode_scales: float32 [384], P('groups'), parts along dimension 0, may hold values from 0.3 to 3
- plane_counts: int32 [32], P(('groups', 'blk')), parts along dimension 0, may hold values from 1 to 2, 20 in all
- links: int32 [32, 2], P(('groups', 'blk')), parts along dimension 0, may hold values from 0 to 1, as said below
Outputs:
- new_modes: bfloat16 [256, 64, 16, 128], P(None, ('groups', 'blk')), parts along dimension 1
- factor: float32 [512, 256], P('groups'), parts along dimension 0
There are 2 independent parts, one for each index of `groups`. A program takes and returns all parts, laid end to end along the dimension named above; each array names one. Nothing has to cross between parts.
Inputs may be any that keep to these rules, and one draw needn't show every extreme that they name: links[b, 1] equals links[b + 1 mod 16, 0]; 1 joins two blocks, 0 is a wall.
All inputs are finite; a program needn't handle non-finite values. No bound on the sum of `plane_counts` on one device may be relied on, other than what follows from the above.
Results may differ from a plain program's by a relative error of at most 0.0095.
Values may be sent and summed in bfloat16 or wider, within the bound.
A program may use at most 128 MiB of HBM per device.

v0:
```python
import jax
import jax.numpy as jnp
from jax import lax
from jax.sharding import PartitionSpec as P


def with_halo(x, sides, width):
    for axis, dim in sides:
        peers, length = (lax.axis_size(axis), x.shape[dim])
        up = [(i, (i + 1) % peers) for i in range(peers)]
        down = [(j, i) for i, j in up]
        last = lax.slice_in_dim(x, length - width, length, axis=dim)
        leading = lax.slice_in_dim(x, 0, width, axis=dim)
        before = lax.ppermute(last, axis, up)
        after = lax.ppermute(leading, axis, down)
        x = jnp.concatenate([before, x, after], axis=dim)
    return x


def smooth_along(field, along):
    widths = [(0, 0)] * field.ndim
    widths[along] = (1, 1)
    padded = jnp.pad(field, widths)
    length = field.shape[along]
    lower = lax.slice_in_dim(padded, 0, length, axis=along)
    upper = lax.slice_in_dim(padded, 2, length + 2, axis=along)
    return 0.25 * lower + 0.5 * field + 0.25 * upper


def gram_term(left_rows, right_rows):
    return lax.dot_general(
        left_rows, right_rows, (((1,), (1,)), ((), ())), preferred_element_type=jnp.float32
    )


def exact_dot(left_mat, right_mat):
    return jnp.dot(left_mat, right_mat, precision=lax.Precision.HIGHEST)


def leaf_factor(matrix):
    order = matrix.shape[0]
    row_ids = lax.iota(jnp.int32, order)
    lower = jnp.zeros((order, order), jnp.float32)
    for column in range(order):
        residue = matrix[:, column] - exact_dot(lower, lower[column, :])
        pivot = jnp.sqrt(residue[column])
        lower = lower.at[:, column].set(jnp.where(row_ids >= column, residue / pivot, 0.0))
    inverse = jnp.zeros((order, order), jnp.float32)
    for row in range(order):
        target = jnp.zeros((order,), jnp.float32).at[row].set(1.0)
        solved = (target - exact_dot(lower[row, :], inverse)) / lower[row, row]
        inverse = inverse.at[row, :].set(solved)
    return (lower, inverse)


def lower_factor(matrix):
    order = matrix.shape[0]
    if order <= 8:
        return leaf_factor(matrix)
    half = order // 2
    lower_one, inverse_one = lower_factor(matrix[:half, :half])
    below = exact_dot(matrix[half:, :half], inverse_one.T)
    rest = matrix[half:, half:] - exact_dot(below, below.T)
    lower_two, inverse_two = lower_factor(rest)
    corner = -exact_dot(inverse_two, exact_dot(below, inverse_one))
    top_zero = jnp.zeros((half, order - half), jnp.float32)
    lower = jnp.concatenate(
        [
            jnp.concatenate([lower_one, top_zero], axis=1),
            jnp.concatenate([below, lower_two], axis=1),
        ],
        axis=0,
    )
    inverse = jnp.concatenate(
        [
            jnp.concatenate([inverse_one, top_zero], axis=1),
            jnp.concatenate([corner, inverse_two], axis=1),
        ],
        axis=0,
    )
    return (lower, inverse)


def shards(snapshots, old_modes, mode_scales, plane_counts, links):
    new_count, plane_slots, rows_y, rows_z = snapshots.shape
    keep_count = old_modes.shape[0]
    columns = new_count + keep_count
    plane_count = plane_counts[0]
    plane_ids = lax.iota(jnp.int32, plane_slots)
    alive_mask = (plane_ids < plane_count).astype(jnp.float32)[None, :, None, None]
    last_pick = (plane_ids == plane_count - 1).astype(jnp.float32)[None, :, None, None]
    masked = snapshots.astype(jnp.float32) * alive_mask
    first_plane = masked[:, 0]
    last_plane = jnp.sum(masked * last_pick, axis=1)
    edge_planes = jnp.stack([first_plane, last_plane], axis=1).astype(jnp.bfloat16)
    widened = with_halo(edge_planes, (("blk", 1),), 1)
    left_halo = widened[:, 0].astype(jnp.float32) * links[0, 0].astype(jnp.float32)
    right_halo = widened[:, 3].astype(jnp.float32) * links[0, 1].astype(jnp.float32)
    behind = jnp.concatenate([left_halo[:, None], masked[:, :-1]], axis=1)
    forward = jnp.concatenate([masked[:, 1:], jnp.zeros_like(masked[:, :1])], axis=1)
    forward = forward + last_pick * right_halo[:, None]
    along_planes = 0.25 * behind + 0.5 * masked + 0.25 * forward
    filtered = (smooth_along(smooth_along(along_planes, 2), 3) * alive_mask).astype(jnp.bfloat16)
    scaled = (mode_scales[:, None, None, None] * old_modes.astype(jnp.float32) * alive_mask).astype(
        jnp.bfloat16
    )
    stacked = jnp.concatenate([filtered, scaled], axis=0).reshape(
        columns, plane_slots * rows_y * rows_z
    )
    cell_total = lax.axis_size("blk") * stacked.shape[1]
    local_gram = gram_term(stacked, stacked)
    gram = lax.psum(local_gram, "blk") / cell_total
    lower, inverse_lower = lower_factor(gram)
    factor = lower.T
    inverse_high = inverse_lower.astype(jnp.bfloat16)
    inverse_low = (inverse_lower - inverse_high.astype(jnp.float32)).astype(jnp.bfloat16)
    result = jnp.dot(inverse_high, stacked, preferred_element_type=jnp.float32)
    result = result + jnp.dot(inverse_low, stacked, preferred_element_type=jnp.float32)
    return (result.reshape(columns, plane_slots, rows_y, rows_z).astype(jnp.bfloat16), factor)


def solution(mesh):
    return jax.shard_map(
        shards,
        mesh=mesh,
        in_specs=(
            P(None, ("groups", "blk"), None, None),
            P(None, ("groups", "blk"), None, None),
            P("groups"),
            P(("groups", "blk")),
            P(("groups", "blk"), None),
        ),
        out_specs=(P(None, ("groups", "blk"), None, None), P("groups", None)),
        check_vma=False,
    )
```

profile of v0, /device:TPU:1, one launch (start us, length us, event | category | flops | bytes accessed | tf_op | source)
XLA Modules:
  0.0 922.4 jit_solution(12888956410553050702)
XLA Ops:
  7.9 1.4 multiply_reduce_fusion
  9.5 2.6 collective-permute-start
  21.0 1.4 convolution_bitcast_fusion
  22.4 1.5 pad_maximum_fusion
  24.0 2.9 copy.589
  26.9 88.4 %all-reduce.131.cloned.1.call-done = f32[256,256]{1,0:T(8,128)} async-done(((f32[256,256]{1,0:T(8,128)}), f32[256,256]{1,0:T(8,128)}) %all-reduce.131.cloned.1.call-update) | async-done | bytes 262160 | tf_op jit(solution)/shard_map/psum | solution.py:112
  115.3 1.0 broadcast_multiply_fusion
  139.7 0.8 fusion.32
  161.9 0.8 fusion.54
  163.5 0.8 fusion.60
  188.9 0.8 fusion.94
  213.2 0.8 fusion.122
  214.0 0.8 fusion.125
  238.9 0.8 fusion.156
  261.0 0.8 fusion.178
  261.9 0.8 fusion.181
  288.0 0.8 fusion.218
  311.2 0.8 fusion.243
  312.8 0.8 fusion.249
  337.3 0.8 fusion.277
  338.1 0.8 fusion.280
  360.3 0.8 fusion.302
  361.9 0.8 fusion.308
  386.5 0.8 fusion.339
  387.3 0.8 fusion.342
  412.0 0.8 fusion.373
  436.8 0.8 fusion.404
  459.2 0.8 fusion.426
  486.2 0.8 fusion.466
  511.2 0.8 fusion.497
  536.7 0.8 fusion.528
  558.9 0.8 fusion.550
  586.3 0.8 fusion.590
  611.0 0.8 fusion.621
  635.8 0.8 fusion.652
  658.0 0.8 fusion.674
  685.0 0.8 fusion.714
  710.0 0.8 fusion.745
  735.1 0.8 fusion.776
  757.3 0.8 fusion.798
  784.3 0.8 fusion.838
  808.9 0.8 fusion.869
  834.1 0.8 fusion.900
  856.3 0.8 fusion.922
  883.4 0.8 fusion.962
  908.9 0.8 fusion.993
  910.1 0.8 copy.591
  913.5 1.8 copy.625
  (2228 shorter events, 610.4 us)
Async XLA Ops:
  7.2 4.9 copy-start.3
  7.2 108.2 %all-reduce.131.cloned.1.call-start = ((), (), s32[]{:S(2)}) async-start(), calls=%async_computation | async-start | bytes 524288 | tf_op jit(solution)/shard_map/psum | solution.py:112
  7.9 4.2 copy-start.1
  9.4 10.2 %collective-permute-start.1 = (bf16[64,1,16,128]{3,0,2,1:T(8,128)(2,1)S(1)}, bf16[64,1,16,128]{3,0,2,1:T(8,128)(2,1)S(1)}, u32[]{:S(2)}, u32[]{:S(2)}) collective-permute-start(bf16[64,1,16,128]{3,0,2,1:T(8,128)(2,1)S(1)} %slice.17541), channel_id=1, source_target_pairs={{1,0},{2,1},{3,2},{4,3},{5,4},{6,5},{7,6},{8,7},{9,8},{10,9},{11,1... | collective-permute-start | bytes 786440 | tf_op jit(solution)/shard_map/ppermute | solution.py:15
  9.5 3.5 copy-start.2
  9.5 10.2 %collective-permute-start = (bf16[64,1,16,128]{3,0,2,1:T(8,128)(2,1)S(1)}, bf16[64,1,16,128]{3,0,2,1:T(8,128)(2,1)S(1)}, u32[]{:S(2)}, u32[]{:S(2)}) collective-permute-start(bf16[64,1,16,128]{3,0,2,1:T(8,128)(2,1)S(1)} %bitcast.7046), channel_id=1, source_target_pairs={{0,1},{1,2},{2,3},{3,4},{4,5},{5,6},{6,7},{7,8},{8,9},{9,10},{10,1... | collective-permute-start | bytes 786440 | tf_op jit(solution)/shard_map/ppermute | solution.py:14
  12.9 6.8 copy-start
  23.9 110.3 %copy-start.11 = (f32[8]{0:T(128)S(1)}, f32[8]{0:T(128)}, u32[]{:S(2)}) copy-start(f32[8]{0:T(128)} %constant.13709.clone.1) | copy-start | bytes 100
  23.9 111.1 %copy-start.10 = (f32[8]{0:T(128)S(1)}, f32[8]{0:T(128)}, u32[]{:S(2)}) copy-start(f32[8]{0:T(128)} %constant.13724.clone.1) | copy-start | bytes 100
  23.9 111.8 %copy-start.9 = (f32[8]{0:T(128)S(1)}, f32[8]{0:T(128)}, u32[]{:S(2)}) copy-start(f32[8]{0:T(128)} %constant.13725.clone.1) | copy-start | bytes 100
  23.9 112.6 %copy-start.8 = (f32[8]{0:T(128)S(1)}, f32[8]{0:T(128)}, u32[]{:S(2)}) copy-start(f32[8]{0:T(128)} %constant.13726.clone.1) | copy-start | bytes 100
  23.9 113.4 %copy-start.7 = (f32[8]{0:T(128)S(1)}, f32[8]{0:T(128)}, u32[]{:S(2)}) copy-start(f32[8]{0:T(128)} %constant.13727.clone.1) | copy-start | bytes 100
  24.0 114.1 %copy-start.6 = (f32[8]{0:T(128)S(1)}, f32[8]{0:T(128)}, u32[]{:S(2)}) copy-start(f32[8]{0:T(128)} %constant.13728.clone.1) | copy-start | bytes 100
  24.0 114.9 %copy-start.5 = (f32[8]{0:T(128)S(1)}, f32[8]{0:T(128)}, u32[]{:S(2)}) copy-start(f32[8]{0:T(128)} %constant.13729.clone.1) | copy-start | bytes 100
  24.0 115.7 %copy-start.4 = (f32[8]{0:T(128)S(1)}, f32[8]{0:T(128)}, u32[]{:S(2)}) copy-start(f32[8]{0:T(128)} %constant.13730.clone.1) | copy-start | bytes 100
Sparse Core Ops, SparseCore 0:
  22.6 92.7 all-reduce.130
where the time goes:
time: 937 us; the launch traced here: 922 us
  matrix products  245 us (26%)
  local copies, waits for them, and re-layouts  242 us (26%)
  between operations  178 us (19%)
  other arithmetic  166 us (18%)
  waiting for transfers between devices  88.4 us (9%)
    dot_general x605, matrix products, exact_dot(): return jnp.dot(left_mat, right_mat, precision=lax.Precision.HIGHEST)  243 us
    another operation x423, other arithmetic  157 us
    slice x224, local copies, waits for them, and re-layouts, leaf_factor(): pivot = jnp.sqrt(residue[column])  134 us
    psum x1, waiting for transfers between devices, shards(): gram = lax.psum(local_gram, 'blk') / cell_total  88.4 us
    slice x64, local copies, waits for them, and re-layouts, leaf_factor(): solved = (target - exact_dot(lower[row, :], inverse)) / lower[row, row]  42.5 us
    scatter x256, local copies, waits for them, and re-layouts, leaf_factor(): lower.at[:, column].set(jnp.where(row_ids >= column, residue / pivot, 0.0))  21.1 us
    another operation x256, local copies, waits for them, and re-layouts  20.9 us
  transfers between devices with their start and end apart: 3, of which 1 were waited for; matrix products, arithmetic and copies ran while one was open for 1% of the time, Pallas kernels for 0%

commit v1 on v0

v1 whole, which is shorter than its diff:
```python
import functools

import jax
import jax.numpy as jnp
from jax import lax
from jax.experimental import pallas as pl
from jax.experimental.pallas import tpu as pltpu
from jax.sharding import PartitionSpec as P

PANEL = 64
VMEM_BYTES = 48 * 1024 * 1024


def stack_kernel(rows_y, snap_ref, modes_ref, scale_ref, left_ref, right_ref, count_ref, link_ref,
                 stacked_ref, gram_ref, snap_tmp, mode_tmp):
    new, planes, _, rows_z = snap_ref.shape
    keep = modes_ref.shape[0]
    alive1 = (count_ref[0] > 1).astype(jnp.float32)
    link0 = link_ref[0, 0].astype(jnp.float32)
    link1 = link_ref[0, 1].astype(jnp.float32)
    lane = lax.broadcasted_iota(jnp.int32, (new, rows_z), 1)

    for p in range(planes):
        alive = jnp.float32(1.0) if p == 0 else alive1
        scaled = modes_ref[:, p].astype(jnp.float32) * (scale_ref[...] * alive)[:, :, None]
        mode_tmp[...] = scaled.reshape(keep * rows_y, rows_z)
        for y in range(rows_y):
            part = mode_tmp[pl.ds(y, keep, stride=rows_y), :]
            at = (p * rows_y + y) * rows_z
            stacked_ref[new:, at:at + rows_z] = part.astype(jnp.bfloat16)

    x0 = snap_ref[:, 0].astype(jnp.float32)
    x1 = snap_ref[:, 1].astype(jnp.float32) * alive1
    right = right_ref[...].astype(jnp.float32) * link1
    left = left_ref[...].astype(jnp.float32) * link0
    along0 = 0.25 * left + 0.5 * x0 + 0.25 * (x1 + (1.0 - alive1) * right)
    along1 = alive1 * (0.25 * x0 + 0.5 * x1 + 0.25 * right)
    for p, along in ((0, along0), (1, along1)):
        snap_tmp[...] = along.reshape(new * rows_y, rows_z)
        lines = [snap_tmp[pl.ds(y, new, stride=rows_y), :] for y in range(rows_y)]
        for y in range(rows_y):
            value = 0.5 * lines[y]
            if y > 0:
                value = value + 0.25 * lines[y - 1]
            if y + 1 < rows_y:
                value = value + 0.25 * lines[y + 1]
            lower = jnp.where(lane == 0, 0.0, pltpu.roll(value, 1, 1))
            upper = jnp.where(lane == rows_z - 1, 0.0, pltpu.roll(value, rows_z - 1, 1))
            value = 0.25 * lower + 0.5 * value + 0.25 * upper
            at = (p * rows_y + y) * rows_z
            stacked_ref[:new, at:at + rows_z] = value.astype(jnp.bfloat16)

    gram_ref[...] = lax.dot_general(
        stacked_ref[...], stacked_ref[...], (((1,), (1,)), ((), ())),
        preferred_element_type=jnp.float32)


def inverse_of(x):
    guess = pl.reciprocal(x, approx=True)
    return guess * (2.0 - x * guess)


def lanes(x, j):
    return jnp.broadcast_to(x[:, j:j + 1], (8, 2 * PANEL))


def leaf(block):
    n = PANEL
    eye = (lax.broadcasted_iota(jnp.int32, (n, n), 0)
           == lax.broadcasted_iota(jnp.int32, (n, n), 1)).astype(jnp.float32)
    work = jnp.concatenate([block, eye], axis=1)
    tiles = [work[8 * t:8 * t + 8] for t in range(n // 8)]
    sub = lax.broadcasted_iota(jnp.int32, (8, 2 * n), 0)
    for j in range(0, n, 2):
        t0, s = divmod(j, 8)
        row0 = jnp.broadcast_to(tiles[t0][s:s + 1], (8, 2 * n))
        row1 = jnp.broadcast_to(tiles[t0][s + 1:s + 2], (8, 2 * n))
        a, b, c = lanes(row0, j), lanes(row0, j + 1), lanes(row1, j + 1)
        scale = inverse_of(a * c - b * b)
        first = (c * row0 - b * row1) * scale
        second = (a * row1 - b * row0) * scale
        for t in range(t0, n // 8):
            step = lanes(tiles[t], j) * first + lanes(tiles[t], j + 1) * second
            if t == t0:
                step = jnp.where(sub > s + 1, step, 0.0)
                step = jnp.where(sub == s + 1, b * inverse_of(a) * row0, step)
            tiles[t] = tiles[t] - step
    work = jnp.concatenate(tiles, axis=0)
    pick = (lax.broadcasted_iota(jnp.int32, (n, 2 * n), 0)
            == lax.broadcasted_iota(jnp.int32, (n, 2 * n), 1))
    diagonal = jnp.sum(jnp.where(pick, work, 0.0), axis=1, keepdims=True)
    work = work * lax.rsqrt(diagonal)
    row = lax.broadcasted_iota(jnp.int32, (n, n), 0)
    col = lax.broadcasted_iota(jnp.int32, (n, n), 1)
    return jnp.where(col >= row, work[:, :n], 0.0), work[:, n:]


def factor_kernel(inv_cells, rows_y, gram_ref, stacked_hbm, out_ref, factor_ref,
                  stacked, packed, inverse, tmp, sem):
    load = pltpu.make_async_copy(stacked_hbm, stacked, sem)
    load.start()
    order = gram_ref.shape[0]
    rows_z = out_ref.shape[3]
    exact = functools.partial(lax.dot_general, precision=lax.Precision.HIGHEST,
                              preferred_element_type=jnp.float32)
    packed[...] = gram_ref[...] * inv_cells
    col = lax.broadcasted_iota(jnp.int32, (1, order), 1)
    for at in range(0, order, PANEL):
        end = at + PANEL
        upper, low_inv = leaf(packed[at:end, at:end])
        inside = (col >= at) & (col < end)
        top = exact(low_inv, packed[at:end, :], (((1,), (0,)), ((), ())))
        spread = jnp.concatenate(
            [low_inv if q == at else jnp.zeros_like(low_inv) for q in range(0, order, PANEL)], axis=1)
        top = jnp.where(inside, spread, top)
        inverse[at:end, :] = jnp.where(col < end, top, 0.0)
        placed = jnp.concatenate(
            [upper if q == at else jnp.zeros_like(upper) for q in range(0, order, PANEL)], axis=1)
        factor_ref[at:end, :] = jnp.where(col >= end, top, placed)
        if end < order:
            update = exact(top[:, end:], top, (((0,), (0,)), ((), ())))
            packed[end:, :] = jnp.where(inside, 0.0, packed[end:, :]) - update

    full = inverse[...]
    high = full.astype(jnp.bfloat16)
    low = (full - high.astype(jnp.float32)).astype(jnp.bfloat16)
    load.wait()
    for p in range(out_ref.shape[1]):
        for y in range(0, rows_y, 2):
            at = (p * rows_y + y) * rows_z
            part = stacked[:, at:at + 2 * rows_z]
            value = (jnp.dot(high, part, preferred_element_type=jnp.float32)
                     + jnp.dot(low, part, preferred_element_type=jnp.float32))
            tmp[pl.ds(y, order, stride=rows_y), :] = value[:, :rows_z]
            tmp[pl.ds(y + 1, order, stride=rows_y), :] = value[:, rows_z:]
        out_ref[:, p] = tmp[...].reshape(order, rows_y, rows_z).astype(jnp.bfloat16)


def shards(snapshots, old_modes, mode_scales, plane_counts, links):
    new, planes, rows_y, rows_z = snapshots.shape
    keep = old_modes.shape[0]
    order = new + keep
    cells = planes * rows_y * rows_z
    peers = lax.axis_size("blk")
    up = [(i, (i + 1) % peers) for i in range(peers)]
    down = [(j, i) for i, j in up]
    first = snapshots[:, 0]
    last = jnp.where(plane_counts[0] > 1, snapshots[:, 1], snapshots[:, 0])
    left = lax.ppermute(last, "blk", up)
    right = lax.ppermute(first, "blk", down)
    vmem = pl.BlockSpec(memory_space=pltpu.VMEM)
    smem = pl.BlockSpec(memory_space=pltpu.SMEM)
    stacked, gram = pl.pallas_call(
        functools.partial(stack_kernel, rows_y),
        out_shape=(jax.ShapeDtypeStruct((order, cells), jnp.bfloat16),
                   jax.ShapeDtypeStruct((order, order), jnp.float32)),
        in_specs=[vmem] * 5 + [smem] * 2,
        out_specs=(vmem, vmem),
        scratch_shapes=[pltpu.VMEM((new * rows_y, rows_z), jnp.float32),
                        pltpu.VMEM((keep * rows_y, rows_z), jnp.float32)],
        compiler_params=pltpu.CompilerParams(vmem_limit_bytes=VMEM_BYTES),
        name="stack",
    )(snapshots, old_modes, mode_scales[:, None], left, right, plane_counts, links)
    gram = lax.psum(gram, "blk")
    new_modes, factor = pl.pallas_call(
        functools.partial(factor_kernel, 1.0 / (peers * cells), rows_y),
        out_shape=(jax.ShapeDtypeStruct((order, planes, rows_y, rows_z), jnp.bfloat16),
                   jax.ShapeDtypeStruct((order, order), jnp.float32)),
        in_specs=[vmem, pl.BlockSpec(memory_space=pl.ANY)],
        out_specs=(vmem, vmem),
        scratch_shapes=[pltpu.VMEM((order, cells), jnp.bfloat16),
                        pltpu.VMEM((order, order), jnp.float32),
                        pltpu.VMEM((order, order), jnp.float32),
                        pltpu.VMEM((order * rows_y, rows_z), jnp.float32),
                        pltpu.SemaphoreType.DMA],
        compiler_params=pltpu.CompilerParams(vmem_limit_bytes=VMEM_BYTES),
        name="factor",
    )(gram, stacked)
    return (new_modes, factor)


def solution(mesh):
    return jax.shard_map(
        shards,
        mesh=mesh,
        in_specs=(
            P(None, ("groups", "blk"), None, None),
            P(None, ("groups", "blk"), None, None),
            P("groups"),
            P(("groups", "blk")),
            P(("groups", "blk"), None),
        ),
        out_specs=(P(None, ("groups", "blk"), None, None), P("groups", None)),
        check_vma=False,
    )
```

time: 937 us -> 151 us (0.16); the launches traced: 922 us -> 150 us
  matrix products: 245 us -> 0 us
  local copies, waits for them, and re-layouts: 242 us -> 5.81 us
  other arithmetic: 166 us -> 1.07 us
  between operations: 178 us -> 14.7 us
  Pallas kernels: 0 us -> 29 us
    dot_general x608 -> x0, matrix products: 245 us -> none  [the longest x605 243 us: exact_dot(): return jnp.dot(left_mat, right_mat, precision=lax.Precision.HIGHEST)]
    slice x323 -> x0, local copies, waits for them, and re-layouts: 188 us -> none  [the longest x224 134 us: leaf_factor(): pivot = jnp.sqrt(residue[column])]
    another operation x423 -> x0, other arithmetic: 157 us -> none
    pallas_call x0 -> x2, Pallas kernels: none -> 29 us  [the longest x1 24.6 us: shards(): pl.pallas_call(functools.partial(factor_kernel, 1.0 / (peers * cells), ro...]
    scatter x512 -> x0, local copies, waits for them, and re-layouts: 27.1 us -> none  [the longest x256 21.1 us: leaf_factor(): lower.at[:, column].set(jnp.where(row_ids >= column, residue / pivot, 0.0))]
    another operation x256 -> x0, local copies, waits for them, and re-layouts: 20.9 us -> none
  transfers between devices with their start and end apart: 3 -> 3, of which waited for: 1 -> 3; matrix products, arithmetic and copies ran while one was open for 1% -> 1% of each run, Pallas kernels for 0% -> 0%
where the time goes in v1:
time: 151 us; the launch traced here: 150 us
  waiting for transfers between devices  97 us (64%)
  Pallas kernels  29 us (19%)
  between operations  14.7 us (10%)
  local copies, waits for them, and re-layouts  5.81 us (4%)
  starting transfers between devices  2.75 us (2%)
    psum x1, waiting for transfers between devices, shards(): gram = lax.psum(gram, 'blk')  92.5 us
    pallas_call x1, Pallas kernels, shards(): pl.pallas_call(functools.partial(factor_kernel, 1.0 / (peers * cells), ro...  24.6 us
    pallas_call x1, Pallas kernels, shards(): pl.pallas_call(functools.partial(stack_kernel, rows_y), out_shape=(jax.Sh...  4.35 us
    unnamed x8, local copies, waits for them, and re-layouts  4.05 us
  transfers between devices with their start and end apart: 3, of which 3 were waited for; matrix products, arithmetic and copies ran while one was open for 1% of the time, Pallas kernels for 0%

profile of v1, /device:TPU:1, one launch (start us, length us, event | category | flops | bytes accessed | tf_op | source)
XLA Modules:
  0.0 150.3 jit_solution(14095223432552849102)
XLA Ops:
  7.2 0.0 all-reduce.2.cloned.1.call-start
  7.2 1.0 slice_bitcast_fusion
  8.2 0.1 collective-permute-start.1
  8.9 1.1 bitcast_select_fusion
  10.0 2.6 %collective-permute-start = (bf16[64,16,128]{2,1,0:T(8,128)(2,1)S(1)}, bf16[64,16,128]{2,1,0:T(8,128)(2,1)S(1)}, u32[]{:S(2)}, u32[]{:S(2)}) collective-permute-start(bf16[64,16,128]{2,1,0:T(8,128)(2,1)S(1)} %bitcast_select_fusion), channel_id=1, source_target_pairs={{0,1},{1,2},{2,3},{3,4},{4,5},{5,6},{6,7},{7,8},{8,9},{9,10},{10,1... | collective-permute-start | bytes 786440 | tf_op jit(solution)/shard_map/ppermute | solution.py:149
  12.6 0.8 copy.11.scale_ref
  13.4 1.5 collective-permute-done.1.right_ref
  14.9 3.0 %collective-permute-done.left_ref = bf16[64,16,128]{2,1,0:T(8,128)(2,1)S(1)} collective-permute-done((bf16[64,16,128]{2,1,0:T(8,128)(2,1)S(1)}, bf16[64,16,128]{2,1,0:T(8,128)(2,1)S(1)}, u32[]{:S(2)}, u32[]{:S(2)}) %collective-permute-start) | collective-permute-done | bytes 262176 | tf_op jit(solution)/shard_map/ppermute | solution.py:149
  17.9 0.0 copy-start
  17.9 1.0 copy-done
  18.9 0.0 copy-start.1
  18.9 1.4 copy-done.1
  20.3 0.0 copy-start.3
  20.3 0.7 copy-done.3
  21.0 4.3 %stack.1 = (bf16[256,4096]{1,0:T(8,128)(2,1)S(1)}, f32[256,256]{1,0:T(8,128)}) custom-call(bf16[64,2,16,128]{3,2,1,0:T(8,128)(2,1)S(1)} %copy-done, bf16[192,2,16,128]{3,2,1,0:T(8,128)(2,1)S(1)} %copy-done.1, f32[192,1]{1,0:T(8,128)S(1)} %copy.11.scale_ref, bf16[64,16,128]{2,1,0:T(8,128)(2,1)S(1)} %collective-permute-done.left_ref, ...), custom_call_target="tpu_custom_call" | custom-call | tf_op jit(solution)/shard_map/stack/pallas_call | solution.py:153
  25.3 0.0 all-reduce.2.cloned.1.call-update
  25.4 92.5 %all-reduce.2.cloned.1.call-done.gram_ref = f32[256,256]{1,0:T(8,128)} async-done(((f32[256,256]{1,0:T(8,128)}), f32[256,256]{1,0:T(8,128)}) %all-reduce.2.cloned.1.call-update) | async-done | bytes 262160 | tf_op jit(solution)/shard_map/psum | solution.py:164
  117.8 0.0 copy-start.2
  117.8 0.9 copy-done.2
  118.8 24.6 %factor.1 = (bf16[256,2,16,128]{3,2,1,0:T(8,128)(2,1)}, f32[256,256]{1,0:T(8,128)}) custom-call(f32[256,256]{1,0:T(8,128)S(1)} %copy-done.2, bf16[256,4096]{1,0:T(8,128)(2,1)S(1)} %get-tuple-element.5.stacked_hbm), custom_call_target="tpu_custom_call" | custom-call | tf_op jit(solution)/shard_map/factor/pallas_call | solution.py:165
Async XLA Ops:
  7.2 110.7 %all-reduce.2.cloned.1.call-start = ((), (), s32[]{:S(2)}) async-start(), calls=%async_computation | async-start | bytes 524288 | tf_op jit(solution)/shard_map/psum | solution.py:164
  8.2 6.7 %collective-permute-start.1 = (bf16[64,16,128]{2,1,0:T(8,128)(2,1)S(1)}, bf16[64,16,128]{2,1,0:T(8,128)(2,1)S(1)}, u32[]{:S(2)}, u32[]{:S(2)}) collective-permute-start(bf16[64,16,128]{2,1,0:T(8,128)(2,1)S(1)} %slice_bitcast_fusion), channel_id=1, source_target_pairs={{1,0},{2,1},{3,2},{4,3},{5,4},{6,5},{7,6},{8,7},{9,8},{10,9},{11,1... | collective-permute-start | bytes 786440 | tf_op jit(solution)/shard_map/ppermute | solution.py:150
  10.0 7.9 %collective-permute-start = (bf16[64,16,128]{2,1,0:T(8,128)(2,1)S(1)}, bf16[64,16,128]{2,1,0:T(8,128)(2,1)S(1)}, u32[]{:S(2)}, u32[]{:S(2)}) collective-permute-start(bf16[64,16,128]{2,1,0:T(8,128)(2,1)S(1)} %bitcast_select_fusion), channel_id=1, source_target_pairs={{0,1},{1,2},{2,3},{3,4},{4,5},{5,6},{6,7},{7,8},{8,9},{9,10},{10,1... | collective-permute-start | bytes 786440 | tf_op jit(solution)/shard_map/ppermute | solution.py:149
  17.9 1.0 copy-start
  18.9 1.4 copy-start.1
  20.3 0.7 copy-start.3
  117.8 0.9 copy-start.2
Sparse Core Ops, SparseCore 0:
  25.5 92.3 all-reduce.1

commit v2 on v1

--- a/solution.py
+++ b/solution.py
@@ -11,28 +11,81 @@
 VMEM_BYTES = 48 * 1024 * 1024
 
 
-def stack_kernel(rows_y, snap_ref, modes_ref, scale_ref, left_ref, right_ref, count_ref, link_ref,
-                 stacked_ref, gram_ref, snap_tmp, mode_tmp):
-    new, planes, _, rows_z = snap_ref.shape
-    keep = modes_ref.shape[0]
+def levels_of(peers, rows):
+    found, stride = [], 1
+    while stride < peers:
+        left = peers // stride
+        radix = next((r for r in (4, 2) if left % r == 0), left)
+        kept = rows // radix if rows % (8 * radix) == 0 else rows
+        found.append((stride, radix, rows, kept))
+        stride, rows = stride * radix, kept
+    return found
+
+
+def stack_kernel(levels, peers, scale_ref, count_ref, link_ref, snap_hbm, modes_hbm,
+                 stacked_ref, gram_ref, snap, modes, last, left_in, right_in, snap_tmp, mode_tmp,
+                 total, load_sem, halo_sem, sum_sem, *buffers):
+    new, planes, rows_y, rows_z = snap.shape
+    keep = modes.shape[0]
+    half = stacked_ref.shape[0] // 2
+    parts = buffers[:len(levels) + 1]
+    inbox = buffers[len(levels) + 1:]
+    me = lax.axis_index("blk")
+
+    load_snap = pltpu.make_async_copy(snap_hbm, snap, load_sem.at[0])
+    load_modes = pltpu.make_async_copy(modes_hbm, modes, load_sem.at[1])
+    load_snap.start()
+    load_modes.start()
+
+    above, below = (me + 1) % peers, (me + peers - 1) % peers
+    partners = [above, below]
+    for stride, radix, _, _ in levels:
+        digit = (me // stride) % radix
+        partners += [me + ((digit + k) % radix - digit) * stride for k in range(1, radix)]
+    barrier = pltpu.get_barrier_semaphore()
+    for partner in partners:
+        pl.semaphore_signal(barrier, inc=1, device_id={"blk": partner},
+                            device_id_type=pl.DeviceIdType.MESH)
+
     alive1 = (count_ref[0] > 1).astype(jnp.float32)
     link0 = link_ref[0, 0].astype(jnp.float32)
     link1 = link_ref[0, 1].astype(jnp.float32)
     lane = lax.broadcasted_iota(jnp.int32, (new, rows_z), 1)
 
+    load_snap.wait()
+    last[...] = (snap[:, 1].astype(jnp.float32) * alive1
+                 + snap[:, 0].astype(jnp.float32) * (1.0 - alive1)).astype(jnp.bfloat16)
+    pl.semaphore_wait(barrier, len(partners))
+    send_up = pltpu.make_async_remote_copy(
+        last, left_in, halo_sem.at[0, 0], halo_sem.at[0, 1],
+        device_id={"blk": above}, device_id_type=pl.DeviceIdType.MESH)
+    send_down = pltpu.make_async_remote_copy(
+        snap.at[:, 0], right_in, halo_sem.at[1, 0], halo_sem.at[1, 1],
+        device_id={"blk": below}, device_id_type=pl.DeviceIdType.MESH)
+    send_up.start()
+    send_down.start()
+
+    eye = (lax.broadcasted_iota(jnp.int32, (keep, keep), 0)
+           == lax.broadcasted_iota(jnp.int32, (keep, keep), 1))
+    scale = jnp.sum(jnp.where(eye, scale_ref[...], 0.0), axis=1, keepdims=True)
+    load_modes.wait()
     for p in range(planes):
-        alive = jnp.float32(1.0) if p == 0 else alive1
-        scaled = modes_ref[:, p].astype(jnp.float32) * (scale_ref[...] * alive)[:, :, None]
-        mode_tmp[...] = scaled.reshape(keep * rows_y, rows_z)
+        mode_tmp[...] = modes[:, p].astype(jnp.float32).reshape(keep * rows_y, rows_z)
+        weight = jnp.broadcast_to(scale if p == 0 else scale * alive1, (keep, rows_z))
         for y in range(rows_y):
-            part = mode_tmp[pl.ds(y, keep, stride=rows_y), :]
+            part = mode_tmp[pl.ds(y, keep, stride=rows_y), :] * weight
             at = (p * rows_y + y) * rows_z
             stacked_ref[new:, at:at + rows_z] = part.astype(jnp.bfloat16)
-
-    x0 = snap_ref[:, 0].astype(jnp.float32)
-    x1 = snap_ref[:, 1].astype(jnp.float32) * alive1
-    right = right_ref[...].astype(jnp.float32) * link1
-    left = left_ref[...].astype(jnp.float32) * link0
+    tail = stacked_ref[half:, :]
+    parts[0][:, 2 * half:] = lax.dot_general(
+        tail, tail, (((1,), (1,)), ((), ())), preferred_element_type=jnp.float32)
+
+    x0 = snap[:, 0].astype(jnp.float32)
+    x1 = snap[:, 1].astype(jnp.float32) * alive1
+    send_up.wait_recv()
+    send_down.wait_recv()
+    right = right_in[...].astype(jnp.float32) * link1
+    left = left_in[...].astype(jnp.float32) * link0
     along0 = 0.25 * left + 0.5 * x0 + 0.25 * (x1 + (1.0 - alive1) * right)
     along1 = alive1 * (0.25 * x0 + 0.5 * x1 + 0.25 * right)
     for p, along in ((0, along0), (1, along1)):
@@ -49,10 +102,58 @@
             value = 0.25 * lower + 0.5 * value + 0.25 * upper
             at = (p * rows_y + y) * rows_z
             stacked_ref[:new, at:at + rows_z] = value.astype(jnp.bfloat16)
-
-    gram_ref[...] = lax.dot_general(
-        stacked_ref[...], stacked_ref[...], (((1,), (1,)), ((), ())),
+    parts[0][:, :2 * half] = lax.dot_general(
+        stacked_ref[:half, :], stacked_ref[...], (((1,), (1,)), ((), ())),
         preferred_element_type=jnp.float32)
+
+    sends, base, bases = [send_up, send_down], 0, [0]
+    for level, (stride, radix, rows, kept) in enumerate(levels):
+        digit = (me // stride) % radix
+        split = kept < rows
+        copies = []
+        for k in range(1, radix):
+            other = (digit + k) % radix
+            start = pl.multiple_of(other * kept, 8) if split else 0
+            copy = pltpu.make_async_remote_copy(
+                parts[level].at[pl.ds(start, kept), :], inbox[level].at[k - 1],
+                sum_sem.at[level, 0, k - 1, 0], sum_sem.at[level, 0, k - 1, 1],
+                device_id={"blk": me + (other - digit) * stride},
+                device_id_type=pl.DeviceIdType.MESH)
+            copy.start()
+            copies.append(copy)
+        own = pl.multiple_of(digit * kept, 8) if split else 0
+        value = parts[level][pl.ds(own, kept), :]
+        for k, copy in enumerate(copies):
+            copy.wait_recv()
+            value = value + inbox[level][k]
+        parts[level + 1][...] = value
+        base = base + own
+        bases.append(base)
+        sends += copies
+
+    kept = levels[-1][3]
+    total[pl.ds(pl.multiple_of(base, 8), kept), :] = parts[-1][...]
+    for level in reversed(range(len(levels))):
+        stride, radix, rows, kept = levels[level]
+        if kept == rows:
+            continue
+        digit = (me // stride) % radix
+        piece = total.at[pl.ds(pl.multiple_of(bases[level + 1], 8), kept), :]
+        copies = []
+        for k in range(1, radix):
+            other = (digit + k) % radix
+            copy = pltpu.make_async_remote_copy(
+                piece, piece, sum_sem.at[level, 1, k - 1, 0], sum_sem.at[level, 1, k - 1, 1],
+                device_id={"blk": me + (other - digit) * stride},
+                device_id_type=pl.DeviceIdType.MESH)
+            copy.start()
+            copies.append(copy)
+        for copy in copies:
+            copy.wait_recv()
+        sends += copies
+    gram_ref[...] = total[...]
+    for copy in sends:
+        copy.wait_send()
 
 
 def inverse_of(x):
@@ -99,11 +200,14 @@
                   stacked, packed, inverse, tmp, sem):
     load = pltpu.make_async_copy(stacked_hbm, stacked, sem)
     load.start()
-    order = gram_ref.shape[0]
+    order = out_ref.shape[0]
     rows_z = out_ref.shape[3]
     exact = functools.partial(lax.dot_general, precision=lax.Precision.HIGHEST,
                               preferred_element_type=jnp.float32)
-    packed[...] = gram_ref[...] * inv_cells
+    half = order // 2
+    packed[:half, :] = gram_ref[:, :order] * inv_cells
+    packed[half:, :half] = jnp.zeros((half, half), jnp.float32)
+    packed[half:, half:] = gram_ref[:, order:] * inv_cells
     col = lax.broadcasted_iota(jnp.int32, (1, order), 1)
     for at in range(0, order, PANEL):
         end = at + PANEL
@@ -142,31 +246,40 @@
     order = new + keep
     cells = planes * rows_y * rows_z
     peers = lax.axis_size("blk")
-    up = [(i, (i + 1) % peers) for i in range(peers)]
-    down = [(j, i) for i, j in up]
-    first = snapshots[:, 0]
-    last = jnp.where(plane_counts[0] > 1, snapshots[:, 1], snapshots[:, 0])
-    left = lax.ppermute(last, "blk", up)
-    right = lax.ppermute(first, "blk", down)
+    levels = levels_of(peers, order // 2)
+    radix = max(level[1] for level in levels)
+    packed = lambda rows: pltpu.VMEM((rows, 3 * order // 2), jnp.float32)
     vmem = pl.BlockSpec(memory_space=pltpu.VMEM)
     smem = pl.BlockSpec(memory_space=pltpu.SMEM)
+    hbm = pl.BlockSpec(memory_space=pl.ANY)
+    plane = pltpu.VMEM((new, rows_y, rows_z), jnp.bfloat16)
     stacked, gram = pl.pallas_call(
-        functools.partial(stack_kernel, rows_y),
+        functools.partial(stack_kernel, levels, peers),
         out_shape=(jax.ShapeDtypeStruct((order, cells), jnp.bfloat16),
-                   jax.ShapeDtypeStruct((order, order), jnp.float32)),
-        in_specs=[vmem] * 5 + [smem] * 2,
+                   jax.ShapeDtypeStruct((order // 2, 3 * order // 2), jnp.float32)),
+        in_specs=[vmem, smem, smem, hbm, hbm],
         out_specs=(vmem, vmem),
-        scratch_shapes=[pltpu.VMEM((new * rows_y, rows_z), jnp.float32),
-                        pltpu.VMEM((keep * rows_y, rows_z), jnp.float32)],
-        compiler_params=pltpu.CompilerParams(vmem_limit_bytes=VMEM_BYTES),
+        scratch_shapes=[pltpu.VMEM(snapshots.shape, jnp.bfloat16),
+                        pltpu.VMEM(old_modes.shape, jnp.bfloat16),
+                        plane, plane, plane,
+                        pltpu.VMEM((new * rows_y, rows_z), jnp.float32),
+                        pltpu.VMEM((keep * rows_y, rows_z), jnp.float32),
+                        packed(order // 2),
+                        pltpu.SemaphoreType.DMA((2,)),
+                        pltpu.SemaphoreType.DMA((2, 2)),
+                        pltpu.SemaphoreType.DMA((len(levels), 2, radix - 1, 2)),
+                        packed(order // 2), *[packed(level[3]) for level in levels],
+                        *[pltpu.VMEM((level[1] - 1, level[3], 3 * order // 2), jnp.float32)
+                          for level in levels]],
+        compiler_params=pltpu.CompilerParams(
+            vmem_limit_bytes=VMEM_BYTES, collective_id=0, has_side_effects=True),
         name="stack",
-    )(snapshots, old_modes, mode_scales[:, None], left, right, plane_counts, links)
-    gram = lax.psum(gram, "blk")
+    )(mode_scales.reshape(1, keep), plane_counts, links, snapshots, old_modes)
     new_modes, factor = pl.pallas_call(
         functools.partial(factor_kernel, 1.0 / (peers * cells), rows_y),
         out_shape=(jax.ShapeDtypeStruct((order, planes, rows_y, rows_z), jnp.bfloat16),
                    jax.ShapeDtypeStruct((order, order), jnp.float32)),
-        in_specs=[vmem, pl.BlockSpec(memory_space=pl.ANY)],
+        in_specs=[vmem, hbm],
         out_specs=(vmem, vmem),
         scratch_shapes=[pltpu.VMEM((order, cells), jnp.bfloat16),
                         pltpu.VMEM((order, order), jnp.float32),

time: 151 us -> 58.5 us (0.39)
  waiting for transfers between devices: 97 us -> 0 us
  Pallas kernels: 29 us -> 53.1 us
  between operations: 14.7 us -> 1.3 us
  starting transfers between devices: 2.75 us -> 0 us
  local copies, waits for them, and re-layouts: 5.81 us -> 3.78 us
    psum x1 -> x0, waiting for transfers between devices: 92.5 us -> none  [shards(): gram = lax.psum(gram, 'blk')]
    pallas_call x1, Pallas kernels: 4.35 us -> 28.5 us  [shards(): pl.pallas_call(functools.partial(stack_kernel, levels, peers), out_shape=...]
    ppermute x2 -> x0, waiting for transfers between devices: 4.46 us -> none  [the longest x1 2.98 us: shards(): left = lax.ppermute(last, 'blk', up)]
    ppermute x2 -> x0, starting transfers between devices: 2.71 us -> none  [the longest x1 2.6 us: shards(): left = lax.ppermute(last, 'blk', up)]
  transfers between devices with their start and end apart: 3 -> 0, of which waited for: 3 -> 0; matrix products, arithmetic and copies ran while one was open for 1% -> 0% of each run, Pallas kernels for 0% -> 0%
where the time goes in v2:
time: 58.5 us; the launch traced here: 58.2 us
  Pallas kernels  53.1 us (91%)
  local copies, waits for them, and re-layouts  3.78 us (6%)
  between operations  1.3 us (2%)
    pallas_call x1, Pallas kernels, shards(): pl.pallas_call(functools.partial(stack_kernel, levels, peers), out_shape=...  28.5 us
    pallas_call x1, Pallas kernels, shards(): pl.pallas_call(functools.partial(factor_kernel, 1.0 / (peers * cells), ro...  24.6 us
    unnamed x8, local copies, waits for them, and re-layouts  3.78 us

profile of v2, /device:TPU:1, one launch (start us, length us, event | category | flops | bytes accessed | tf_op | source)
XLA Modules:
  0.0 58.2 jit_solution(7735133410533159966)
XLA Ops:
  1.3 0.0 copy-start
  1.3 1.4 %copy-done = bf16[192,2,16,128]{3,2,1,0:T(8,128)(2,1)S(1)} copy-done((bf16[192,2,16,128]{3,2,1,0:T(8,128)(2,1)S(1)}, bf16[192,2,16,128]{3,2,1,0:T(8,128)(2,1)}, u32[]{:S(2)}) %copy-start) | copy-done | bytes 1572888
  2.7 0.0 copy-start.1
  2.7 1.0 %copy-done.1 = bf16[64,2,16,128]{3,2,1,0:T(8,128)(2,1)S(1)} copy-done((bf16[64,2,16,128]{3,2,1,0:T(8,128)(2,1)S(1)}, bf16[64,2,16,128]{3,2,1,0:T(8,128)(2,1)}, u32[]{:S(2)}) %copy-start.1) | copy-done | bytes 524312
  3.7 0.0 copy-start.2
  3.7 0.7 %copy-done.2 = f32[192]{0:T(256)S(1)} copy-done((f32[192]{0:T(256)S(1)}, f32[192]{0:T(256)}, u32[]{:S(2)}) %copy-start.2) | copy-done | bytes 792
  4.4 0.0 copy-start.3
  4.4 0.7 %copy-done.3 = s32[1,2]{1,0:T(1,128)S(1)} copy-done((s32[1,2]{1,0:T(1,128)S(1)}, s32[1,2]{1,0:T(1,128)}, u32[]{:S(2)}) %copy-start.3) | copy-done | bytes 32
  5.1 28.5 %stack.1 = (bf16[256,4096]{1,0:T(8,128)(2,1)S(1)}, f32[128,384]{1,0:T(8,128)S(1)}) custom-call(f32[1,192]{1,0:T(1,128)S(1)} %bitcast.1, s32[1]{0:T(128)S(6)} %copy.7.count_ref, s32[1,2]{1,0:T(1,128)S(1)} %copy-done.3, bf16[64,2,16,128]{3,2,1,0:T(8,128)(2,1)S(1)} %copy-done.1, bf16[192,2,16,128]{3,2,1,0:T(8,128)(2,1)S(1)} %copy-done), custom_call_target="tpu_custom_call" | custom-call | tf_op jit(solution)/shard_map/stack/pallas_call | solution.py:256
  33.6 24.6 %factor.1 = (bf16[256,2,16,128]{3,2,1,0:T(8,128)(2,1)}, f32[256,256]{1,0:T(8,128)}) custom-call(f32[128,384]{1,0:T(8,128)S(1)} %get-tuple-element.4.gram_ref, bf16[256,4096]{1,0:T(8,128)(2,1)S(1)} %get-tuple-element.5.stacked_hbm), custom_call_target="tpu_custom_call" | custom-call | tf_op jit(solution)/shard_map/factor/pallas_call | solution.py:278
Async XLA Ops:
  1.3 1.4 %copy-start = (bf16[192,2,16,128]{3,2,1,0:T(8,128)(2,1)S(1)}, bf16[192,2,16,128]{3,2,1,0:T(8,128)(2,1)}, u32[]{:S(2)}) copy-start(bf16[192,2,16,128]{3,2,1,0:T(8,128)(2,1)} %modes_hbm.1) | copy-start | bytes 4718596
  2.7 1.0 %copy-start.1 = (bf16[64,2,16,128]{3,2,1,0:T(8,128)(2,1)S(1)}, bf16[64,2,16,128]{3,2,1,0:T(8,128)(2,1)}, u32[]{:S(2)}) copy-start(bf16[64,2,16,128]{3,2,1,0:T(8,128)(2,1)} %snap_hbm.1) | copy-start | bytes 1572868
  3.7 0.7 %copy-start.2 = (f32[192]{0:T(256)S(1)}, f32[192]{0:T(256)}, u32[]{:S(2)}) copy-start(f32[192]{0:T(256)} %param.7) | copy-start | bytes 2308
  4.4 0.7 %copy-start.3 = (s32[1,2]{1,0:T(1,128)S(1)}, s32[1,2]{1,0:T(1,128)}, u32[]{:S(2)}) copy-start(s32[1,2]{1,0:T(1,128)} %link_ref.1) | copy-start | bytes 28

commit v3 on v2

v3 whole, which is shorter than its diff:
```python
import functools

import jax
import jax.numpy as jnp
from jax import lax
from jax.experimental import pallas as pl
from jax.experimental.pallas import tpu as pltpu
from jax.sharding import PartitionSpec as P

PANEL = 64
VMEM_BYTES = 62 * 1024 * 1024


def levels_of(peers, rows):
    found, stride = [], 1
    while stride < peers:
        left = peers // stride
        radix = next((r for r in (4, 2) if left % r == 0), left)
        kept = rows // radix if rows % (8 * radix) == 0 else rows
        found.append((stride, radix, rows, kept))
        stride, rows = stride * radix, kept
    return found


class Exchange:
    def __init__(self, levels, me, parts, inbox, total, sems):
        self.levels, self.me = levels, me
        self.parts, self.inbox, self.total, self.sems = parts, inbox, total, sems
        self.stages = [(level, 0) for level in range(len(levels))]
        self.stages += [(level, 1) for level in reversed(range(len(levels)))
                        if levels[level][3] < levels[level][2]]
        self.base = [0]
        for stride, radix, rows, kept in levels:
            own = ((me // stride) % radix) * kept if kept < rows else 0
            self.base.append(self.base[-1] + own)
        self.at, self.copies, self.sends = 0, [], []

    def start(self):
        level, phase = self.stages[self.at]
        stride, radix, rows, kept = self.levels[level]
        digit = (self.me // stride) % radix
        if phase == 1 and not self.stages[self.at - 1][1]:
            first = pl.multiple_of(self.base[-1], 8)
            self.total[pl.ds(first, self.levels[-1][3]), :] = self.parts[-1][...]
        self.copies = []
        for k in range(1, radix):
            other = (digit + k) % radix
            if phase == 0:
                first = pl.multiple_of(other * kept, 8) if kept < rows else 0
                source = self.parts[level].at[pl.ds(first, kept), :]
                target = self.inbox[level].at[k - 1]
            else:
                first = pl.multiple_of(self.base[level + 1], 8)
                source = target = self.total.at[pl.ds(first, kept), :]
            copy = pltpu.make_async_remote_copy(
                source, target, self.sems.at[level, phase, k - 1, 0],
                self.sems.at[level, phase, k - 1, 1],
                device_id={"blk": self.me + (other - digit) * stride},
                device_id_type=pl.DeviceIdType.MESH)
            copy.start()
            self.copies.append(copy)
        self.sends += self.copies

    def finish(self):
        level, phase = self.stages[self.at]
        stride, radix, rows, kept = self.levels[level]
        if phase == 0:
            own = pl.multiple_of(((self.me // stride) % radix) * kept, 8) if kept < rows else 0
            value = self.parts[level][pl.ds(own, kept), :]
        for k, copy in enumerate(self.copies):
            copy.wait_recv()
            if phase == 0:
                value = value + self.inbox[level][k]
        if phase == 0:
            self.parts[level + 1][...] = value
        self.at += 1

    def advance(self):
        if self.at < len(self.stages):
            self.finish()
            if self.at < len(self.stages):
                self.start()


def stack_kernel(levels, peers, scale_hbm, count_hbm, link_hbm, snap_hbm, modes_hbm,
                 stacked_hbm, gram_new, gram_old, scale_ref, count_ref, link_ref, snap, modes, last, left_in, right_in, snap_tmp, mode_tmp,
                 stacked_ref, total_new, total_old, load_sem, halo_sem, sum_sem, *buffers):
    new, planes, rows_y, rows_z = snap.shape
    keep = modes.shape[0]
    me = lax.axis_index("blk")
    count = 2 * len(levels) + 1
    old_sum, new_sum = [
        Exchange(levels, me, buffers[i * count:i * count + len(levels) + 1],
                 buffers[i * count + len(levels) + 1:(i + 1) * count], total, sum_sem.at[i])
        for i, total in enumerate((total_old, total_new))]

    load_snap = pltpu.make_async_copy(snap_hbm, snap, load_sem.at[0])
    load_modes = pltpu.make_async_copy(modes_hbm, modes, load_sem.at[1])
    small = [pltpu.make_async_copy(source, target, load_sem.at[2 + i]) for i, (source, target) in
             enumerate(((count_hbm, count_ref), (link_hbm, link_ref), (scale_hbm, scale_ref)))]
    load_snap.start()
    for copy in small:
        copy.start()
    load_modes.start()

    above, below = (me + 1) % peers, (me + peers - 1) % peers
    partners = [above, below]
    for stride, radix, _, _ in levels:
        digit = (me // stride) % radix
        partners += [me + ((digit + k) % radix - digit) * stride for k in range(1, radix)]
    barrier = pltpu.get_barrier_semaphore()
    for partner in partners:
        pl.semaphore_signal(barrier, inc=1, device_id={"blk": partner},
                            device_id_type=pl.DeviceIdType.MESH)

    for copy in small:
        copy.wait()
    alive1 = (count_ref[0] > 1).astype(jnp.float32)
    link0 = link_ref[0, 0].astype(jnp.float32)
    link1 = link_ref[0, 1].astype(jnp.float32)
    lane = lax.broadcasted_iota(jnp.int32, (new, rows_z), 1)

    load_snap.wait()
    last[...] = (snap[:, 1].astype(jnp.float32) * alive1
                 + snap[:, 0].astype(jnp.float32) * (1.0 - alive1)).astype(jnp.bfloat16)
    pl.semaphore_wait(barrier, len(partners))
    send_up = pltpu.make_async_remote_copy(
        last, left_in, halo_sem.at[0, 0], halo_sem.at[0, 1],
        device_id={"blk": above}, device_id_type=pl.DeviceIdType.MESH)
    send_down = pltpu.make_async_remote_copy(
        snap.at[:, 0], right_in, halo_sem.at[1, 0], halo_sem.at[1, 1],
        device_id={"blk": below}, device_id_type=pl.DeviceIdType.MESH)
    send_up.start()
    send_down.start()

    eye = (lax.broadcasted_iota(jnp.int32, (keep, keep), 0)
           == lax.broadcasted_iota(jnp.int32, (keep, keep), 1))
    scale = jnp.sum(jnp.where(eye, scale_ref[...], 0.0), axis=1, keepdims=True)
    load_modes.wait()
    for p in range(planes):
        mode_tmp[...] = modes[:, p].astype(jnp.float32).reshape(keep * rows_y, rows_z)
        weight = jnp.broadcast_to(scale if p == 0 else scale * alive1, (keep, rows_z))
        for y in range(rows_y):
            part = mode_tmp[pl.ds(y, keep, stride=rows_y), :] * weight
            at = (p * rows_y + y) * rows_z
            stacked_ref[new:, at:at + rows_z] = part.astype(jnp.bfloat16)
    store_old = pltpu.make_async_copy(
        stacked_ref.at[pl.ds(new, keep), :], stacked_hbm.at[pl.ds(new, keep), :], load_sem.at[5])
    store_old.start()
    tail = stacked_ref[new:, :]
    gram = lax.dot_general(
        tail, tail, (((1,), (1,)), ((), ())), preferred_element_type=jnp.float32)
    at = 0
    for row in range(0, keep, new):
        old_sum.parts[0][:, at:at + keep - row] = gram[row:row + new, row:]
        at += keep - row
    old_sum.start()
    old_sum.advance()

    x0 = snap[:, 0].astype(jnp.float32)
    x1 = snap[:, 1].astype(jnp.float32) * alive1
    send_up.wait_recv()
    send_down.wait_recv()
    right = right_in[...].astype(jnp.float32) * link1
    left = left_in[...].astype(jnp.float32) * link0
    along0 = 0.25 * left + 0.5 * x0 + 0.25 * (x1 + (1.0 - alive1) * right)
    along1 = alive1 * (0.25 * x0 + 0.5 * x1 + 0.25 * right)
    for p, along in ((0, along0), (1, along1)):
        snap_tmp[...] = along.reshape(new * rows_y, rows_z)
        lines = [snap_tmp[pl.ds(y, new, stride=rows_y), :] for y in range(rows_y)]
        for y in range(rows_y):
            value = 0.5 * lines[y]
            if y > 0:
                value = value + 0.25 * lines[y - 1]
            if y + 1 < rows_y:
                value = value + 0.25 * lines[y + 1]
            lower = jnp.where(lane == 0, 0.0, pltpu.roll(value, 1, 1))
            upper = jnp.where(lane == rows_z - 1, 0.0, pltpu.roll(value, rows_z - 1, 1))
            value = 0.25 * lower + 0.5 * value + 0.25 * upper
            at = (p * rows_y + y) * rows_z
            stacked_ref[:new, at:at + rows_z] = value.astype(jnp.bfloat16)
    store_new = pltpu.make_async_copy(
        stacked_ref.at[pl.ds(0, new), :], stacked_hbm.at[pl.ds(0, new), :], load_sem.at[6])
    store_new.start()
    new_sum.parts[0][...] = lax.dot_general(
        stacked_ref[:new, :], stacked_ref[...], (((1,), (1,)), ((), ())),
        preferred_element_type=jnp.float32)
    new_sum.start()
    for _ in new_sum.stages:
        old_sum.advance()
        new_sum.advance()
    gram_new[...] = total_new[...]
    gram_old[...] = total_old[...]
    for copy in (send_up, send_down, *old_sum.sends, *new_sum.sends):
        copy.wait_send()
    store_old.wait()
    store_new.wait()


def inverse_of(x):
    guess = pl.reciprocal(x, approx=True)
    return guess * (2.0 - x * guess)


def lanes(x, j):
    return jnp.broadcast_to(x[:, j:j + 1], (8, 2 * PANEL))


def leaf(block):
    n = PANEL
    eye = (lax.broadcasted_iota(jnp.int32, (n, n), 0)
           == lax.broadcasted_iota(jnp.int32, (n, n), 1)).astype(jnp.float32)
    work = jnp.concatenate([block, eye], axis=1)
    tiles = [work[8 * t:8 * t + 8] for t in range(n // 8)]
    sub = lax.broadcasted_iota(jnp.int32, (8, 2 * n), 0)
    for t0 in range(n // 8):
        at = 8 * t0
        rows = [jnp.broadcast_to(tiles[t0][k:k + 1], (8, 2 * n)) for k in range(8)]
        pivots = [[lanes(rows[k], at + q) if q >= k else None for q in range(8)] for k in range(8)]
        others = range(t0 + 1, n // 8)
        sides = {t: [lanes(tiles[t], at + q) for q in range(8)] for t in others}
        for k in range(0, 8, 2):
            a, b, c = pivots[k][k], pivots[k][k + 1], pivots[k + 1][k + 1]
            scale = inverse_of(a * c - b * b)
            first = {q: (c * pivots[k][q] - b * pivots[k + 1][q]) * scale for q in range(k + 2, 8)}
            second = {q: (a * pivots[k + 1][q] - b * pivots[k][q]) * scale for q in range(k + 2, 8)}
            row_first = (c * rows[k] - b * rows[k + 1]) * scale
            row_second = (a * rows[k + 1] - b * rows[k]) * scale
            for r in range(k + 2, 8):
                x, y = pivots[k][r], pivots[k + 1][r]
                for q in range(r, 8):
                    pivots[r][q] = pivots[r][q] - (x * first[q] + y * second[q])
                rows[r] = rows[r] - (x * row_first + y * row_second)
            for t in others:
                x, y = sides[t][k], sides[t][k + 1]
                for q in range(k + 2, 8):
                    sides[t][q] = sides[t][q] - (x * first[q] + y * second[q])
                tiles[t] = tiles[t] - (x * row_first + y * row_second)
            rows[k + 1] = rows[k + 1] - b * inverse_of(a) * rows[k]
        done = rows[0]
        for k in range(1, 8):
            done = jnp.where(sub == k, rows[k], done)
        tiles[t0] = done
    work = jnp.concatenate(tiles, axis=0)
    pick = (lax.broadcasted_iota(jnp.int32, (n, 2 * n), 0)
            == lax.broadcasted_iota(jnp.int32, (n, 2 * n), 1))
    diagonal = jnp.sum(jnp.where(pick, work, 0.0), axis=1, keepdims=True)
    work = work * lax.rsqrt(diagonal)
    row = lax.broadcasted_iota(jnp.int32, (n, n), 0)
    col = lax.broadcasted_iota(jnp.int32, (n, n), 1)
    return jnp.where(col >= row, work[:, :n], 0.0), work[:, n:]


def factor_kernel(inv_cells, gram_new, gram_old, stacked_hbm, out_hbm, factor_ref,
                  stacked, packed, inverse, tmp, stage, sem):
    load = pltpu.make_async_copy(stacked_hbm, stacked, sem.at[0])
    load.start()
    order, planes, rows_y, rows_z = out_hbm.shape
    new = gram_new.shape[0]
    exact = functools.partial(lax.dot_general, precision=lax.Precision.HIGHEST,
                              preferred_element_type=jnp.float32)
    packed[:new, :] = gram_new[...] * inv_cells
    packed[new:, :] = jnp.zeros((order - new, order), jnp.float32)
    at = 0
    for row in range(new, order, new):
        packed[row:row + new, row:] = gram_old[:, at:at + order - row] * inv_cells
        at += order - row
    col = lax.broadcasted_iota(jnp.int32, (1, order), 1)
    for at in range(0, order, PANEL):
        end = at + PANEL
        upper, low_inv = leaf(packed[at:end, at:end])
        inside = (col >= at) & (col < end)
        top = exact(low_inv, packed[at:end, :], (((1,), (0,)), ((), ())))
        spread = jnp.concatenate(
            [low_inv if q == at else jnp.zeros_like(low_inv) for q in range(0, order, PANEL)], axis=1)
        top = jnp.where(inside, spread, top)
        inverse[at:end, :] = jnp.where(col < end, top, 0.0)
        placed = jnp.concatenate(
            [upper if q == at else jnp.zeros_like(upper) for q in range(0, order, PANEL)], axis=1)
        factor_ref[at:end, :] = jnp.where(col >= end, top, placed)
        if end < order:
            update = exact(top[:, end:], top, (((0,), (0,)), ((), ())))
            packed[end:, :] = jnp.where(inside, 0.0, packed[end:, :]) - update

    full = inverse[...]
    high = full.astype(jnp.bfloat16)
    low = (full - high.astype(jnp.float32)).astype(jnp.bfloat16)
    load.wait()
    stores = []
    for p in range(planes):
        for y in range(0, rows_y, 2):
            at = (p * rows_y + y) * rows_z
            part = stacked[:, at:at + 2 * rows_z]
            value = (jnp.dot(high, part, preferred_element_type=jnp.float32)
                     + jnp.dot(low, part, preferred_element_type=jnp.float32))
            tmp[pl.ds(y, order, stride=rows_y), :] = value[:, :rows_z]
            tmp[pl.ds(y + 1, order, stride=rows_y), :] = value[:, rows_z:]
        stage[p] = tmp[...].reshape(order, rows_y, rows_z).astype(jnp.bfloat16)
        store = pltpu.make_async_copy(stage.at[p], out_hbm.at[:, p], sem.at[1 + p])
        store.start()
        stores.append(store)
    for store in stores:
        store.wait()


def shards(snapshots, old_modes, mode_scales, plane_counts, links):
    new, planes, rows_y, rows_z = snapshots.shape
    keep = old_modes.shape[0]
    order = new + keep
    cells = planes * rows_y * rows_z
    peers = lax.axis_size("blk")
    levels = levels_of(peers, new)
    radix = max(level[1] for level in levels)
    widths = (sum(range(new, keep + 1, new)), order)
    sums = [pltpu.VMEM(shape, jnp.float32) for width in widths for shape in (
        [(new, width)] + [(level[3], width) for level in levels]
        + [(level[1] - 1, level[3], width) for level in levels])]
    vmem = pl.BlockSpec(memory_space=pltpu.VMEM)
    smem = pl.BlockSpec(memory_space=pltpu.SMEM)
    hbm = pl.BlockSpec(memory_space=pltpu.HBM)
    plane = pltpu.VMEM((new, rows_y, rows_z), jnp.bfloat16)
    stacked, gram_new, gram_old = pl.pallas_call(
        functools.partial(stack_kernel, levels, peers),
        out_shape=(jax.ShapeDtypeStruct((order, cells), jnp.bfloat16),
                   jax.ShapeDtypeStruct((new, widths[1]), jnp.float32),
                   jax.ShapeDtypeStruct((new, widths[0]), jnp.float32)),
        in_specs=[hbm] * 5,
        out_specs=(hbm, vmem, vmem),
        scratch_shapes=[pltpu.VMEM((1, keep), jnp.float32),
                        pltpu.SMEM(plane_counts.shape, jnp.int32),
                        pltpu.SMEM(links.shape, jnp.int32),
                        pltpu.VMEM(snapshots.shape, jnp.bfloat16),
                        pltpu.VMEM(old_modes.shape, jnp.bfloat16),
                        plane, plane, plane,
                        pltpu.VMEM((new * rows_y, rows_z), jnp.float32),
                        pltpu.VMEM((keep * rows_y, rows_z), jnp.float32),
                        pltpu.VMEM((order, cells), jnp.bfloat16),
                        pltpu.VMEM((new, widths[1]), jnp.float32),
                        pltpu.VMEM((new, widths[0]), jnp.float32),
                        pltpu.SemaphoreType.DMA((7,)),
                        pltpu.SemaphoreType.DMA((2, 2)),
                        pltpu.SemaphoreType.DMA((2, len(levels), 2, radix - 1, 2)), *sums],
        compiler_params=pltpu.CompilerParams(
            vmem_limit_bytes=VMEM_BYTES, collective_id=0, has_side_effects=True),
        name="stack",
    )(mode_scales.reshape(1, keep), plane_counts, links, snapshots, old_modes)
    new_modes, factor = pl.pallas_call(
        functools.partial(factor_kernel, 1.0 / (peers * cells)),
        out_shape=(jax.ShapeDtypeStruct((order, planes, rows_y, rows_z), jnp.bfloat16),
                   jax.ShapeDtypeStruct((order, order), jnp.float32)),
        in_specs=[vmem, vmem, hbm],
        out_specs=(hbm, vmem),
        scratch_shapes=[pltpu.VMEM((order, cells), jnp.bfloat16),
                        pltpu.VMEM((order, order), jnp.float32),
                        pltpu.VMEM((order, order), jnp.float32),
                        pltpu.VMEM((order * rows_y, rows_z), jnp.float32),
                        pltpu.VMEM((planes, order, rows_y, rows_z), jnp.bfloat16),
                        pltpu.SemaphoreType.DMA((1 + planes,))],
        compiler_params=pltpu.CompilerParams(vmem_limit_bytes=VMEM_BYTES),
        name="factor",
    )(gram_new, gram_old, stacked)
    return (new_modes, factor)


def solution(mesh):
    return jax.shard_map(
        shards,
        mesh=mesh,
        in_specs=(
            P(None, ("groups", "blk"), None, None),
            P(None, ("groups", "blk"), None, None),
            P("groups"),
            P(("groups", "blk")),
            P(("groups", "blk"), None),
        ),
        out_specs=(P(None, ("groups", "blk"), None, None), P("groups", None)),
        check_vma=False,
    )
```

time: 58.5 us -> 43.3 us (0.74)
  Pallas kernels: 53.1 us -> 41.5 us
  local copies, waits for them, and re-layouts: 3.78 us -> 0 us
    pallas_call x1, Pallas kernels: 24.6 us -> 16.3 us  [shards(): pl.pallas_call(functools.partial(factor_kernel, 1.0 / (peers * cells)), o...]
    unnamed x8 -> x0, local copies, waits for them, and re-layouts: 3.78 us -> none
    pallas_call x1, Pallas kernels: 28.5 us -> 25.2 us  [shards(): pl.pallas_call(functools.partial(stack_kernel, levels, peers), out_shape=...]
where the time goes in v3:
time: 43.3 us; the launch traced here: 42.8 us
  Pallas kernels  41.5 us (96%)
  between operations  1.29 us (3%)
    pallas_call x1, Pallas kernels, shards(): pl.pallas_call(functools.partial(stack_kernel, levels, peers), out_shape=...  25.2 us
    pallas_call x1, Pallas kernels, shards(): pl.pallas_call(functools.partial(factor_kernel, 1.0 / (peers * cells)), o...  16.3 us

profile of v3, /device:TPU:1, one launch (start us, length us, event | category | flops | bytes accessed | tf_op | source)
XLA Modules:
  0.0 42.8 jit_solution(16425832874103509544)
XLA Ops:
  1.3 25.2 %stack.1 = (bf16[256,4096]{1,0:T(8,128)(2,1)}, f32[64,256]{1,0:T(8,128)}, f32[64,384]{1,0:T(8,128)}) custom-call(f32[1,192]{1,0:T(1,128)} %bitcast.1, s32[1]{0:T(128)S(6)} %copy.7.count_hbm, s32[1,2]{1,0:T(1,128)} %link_hbm.1, bf16[64,2,16,128]{3,2,1,0:T(8,128)(2,1)} %snap_hbm.1, bf16[192,2,16,128]{3,2,1,0:T(8,128)(2,1)} %modes_hbm.1), custom_call_target="tpu_custom_call" | custom-call | tf_op jit(solution)/shard_map/stack/pallas_call | solution.py:322
  26.5 16.3 %factor.1 = (bf16[256,2,16,128]{3,2,1,0:T(8,128)(2,1)}, f32[256,256]{1,0:T(8,128)}) custom-call(f32[64,256]{1,0:T(8,128)} %get-tuple-element.5.gram_new, f32[64,384]{1,0:T(8,128)} %get-tuple-element.6.gram_old, bf16[256,4096]{1,0:T(8,128)(2,1)} %get-tuple-element.7.stacked_hbm), custom_call_target="tpu_custom_call" | custom-call | tf_op jit(solution)/shard_map/factor/pallas_call | solution.py:347
